TPU v7x, 32 devices: a whole 2x2x4 slice. The times are simulated.
32 devices in a mesh: radial: 4 (over y, core), lateral: 8 (over z, x).
Axes of the slice: x: 2, y: 2, z: 4, core: 2. Of those that a mesh axis runs over, the one named last changes fastest.
Arguments:
- pressure: float32 [128, 32, 512], P('radial', 'lateral'), may hold values from -6 to 6
- residual: float32 [128, 32, 512], P('radial', 'lateral'), may hold values from -45 to 45
- inv_visc: float32 [128, 32, 512], P('radial', 'lateral'), may hold values from 0.1 to 10
- thermal: float32 [128, 32, 512], P('radial', 'lateral'), may hold values from -6 to 6
- compress: float32 [128], P('radial'), may hold values from 0.3 to 3
- legendre: bfloat16 [32, 256, 256], P('lateral'), may hold values from -1.5 to 1.5
- kernels: float32 [2, 128, 256], P(None, 'radial'), may hold values from -0.5 to 0.5
Outputs:
- pressure_new: float32 [128, 32, 512], P('radial', 'lateral')
- residual_new: float32 [128, 32, 512], P('radial', 'lateral')
- geoid_coef: float32 [256, 2, 256], P('lateral')
- topo_coef: float32 [256, 2, 256], P('lateral')
All inputs are finite; a program needn't handle non-finite values.
Results may differ from a plain program's by a relative error of at most 0.0051.
Values may be sent and summed in bfloat16 or wider, within the bound.
A program may use at most 128 MiB of HBM per device.

v0:
```python
import math

import jax
import jax.numpy as jnp
from jax import lax
from jax.sharding import PartitionSpec as P


def padded_2(shard, sides, width):
    for axis, dim in sides:
        devices, length = (lax.axis_size(axis), shard.shape[dim])
        up = [(i, (i + 1) % devices) for i in range(devices - 1)]
        down = [(j, i) for i, j in up]
        last = lax.slice_in_dim(shard, length - width, length, axis=dim)
        first = lax.slice_in_dim(shard, 0, width, axis=dim)
        before = lax.ppermute(last, axis, up)
        after = lax.ppermute(first, axis, down)
        shard = jnp.concatenate([before, shard, after], axis=dim)
    return shard


def fourier_table(nlon, orders):
    column = jnp.arange(nlon, dtype=jnp.int32)[:, None]
    order = jnp.arange(orders, dtype=jnp.int32)[None, :]
    phase = 2.0 * math.pi / nlon * (column * order % nlon).astype(jnp.float32)
    scale = 1.0 / math.sqrt(nlon)
    return (jnp.concatenate([jnp.cos(phase), jnp.sin(phase)], axis=1) * scale).astype(jnp.bfloat16)


def on_device(pressure, residual, inv_visc, thermal, compress, legendre, kernels):
    padded = padded_2(residual, (("radial", 0), ("lateral", 1)), 1)
    beside = padded[2:, 1:-1] + padded[:-2, 1:-1] + padded[1:-1, 2:] + padded[1:-1, :-2]
    beside = beside + jnp.roll(residual, 1, axis=2) + jnp.roll(residual, -1, axis=2)
    image = (6.0 + inv_visc) * residual - beside
    squares, curvature = lax.psum(
        (jnp.sum(residual * residual), jnp.sum(residual * image)), ("radial", "lateral")
    )
    alpha = squares / curvature
    pressure_new = pressure + alpha * residual
    residual_new = residual - alpha * image
    anomaly = (thermal - compress[:, None, None] * pressure_new).astype(jnp.bfloat16)
    shells, cycles, nlon = anomaly.shape
    orders = legendre.shape[2]
    owned = legendre.shape[1] // lax.axis_size("lateral")
    table = fourier_table(nlon, orders)
    spectrum = jnp.dot(
        anomaly.reshape(shells * cycles, nlon), table, preferred_element_type=jnp.float32
    )
    spectrum = spectrum.astype(jnp.bfloat16).reshape(shells, cycles, 2, orders)
    table_local = lax.all_to_all(legendre, "lateral", split_axis=1, concat_axis=0, tiled=True)
    coefficients = jnp.einsum(
        "satm,alm->lstm",
        lax.all_gather(spectrum, "lateral", axis=1, tiled=True),
        table_local,
        preferred_element_type=jnp.float32,
    )
    first = lax.axis_index("lateral") * owned
    weights = lax.dynamic_slice_in_dim(kernels, first, owned, 2)
    partial_terms = jnp.einsum(
        "ksl,lstm->lktm", weights, coefficients, precision=lax.Precision.HIGHEST
    )
    response = lax.psum(partial_terms, "radial")
    return (pressure_new, residual_new, response[:, 0], response[:, 1])


def solution(mesh):
    return jax.shard_map(
        on_device,
        mesh=mesh,
        in_specs=(
            P("radial", "lateral", None),
            P("radial", "lateral", None),
            P("radial", "lateral", None),
            P("radial", "lateral", None),
            P("radial"),
            P("lateral", None, None),
            P(None, "radial", None),
        ),
        out_specs=(
            P("radial", "lateral", None),
            P("radial", "lateral", None),
            P("lateral", None, None),
            P("lateral", None, None),
        ),
        check_vma=False,
    )
```

profile of v0, /device:TPU:0, one launch (start us, length us, event | category | flops | bytes accessed | tf_op | source)
XLA Modules:
  0.0 179.3 jit_solution(15585047494259726712)
XLA Ops:
  7.2 0.8 fusion.23
  8.0 2.3 %collective-permute-start.1 = (f32[1,4,512]{2,1,0:T(4,128)S(1)}, f32[1,4,512]{2,1,0:T(4,128)S(1)}, u32[]{:S(2)}, u32[]{:S(2)}) collective-permute-start(f32[1,4,512]{2,1,0:T(4,128)S(1)} %get-tuple-element.15), channel_id=1, source_target_pairs={{0,8},{8,16},{16,24},{1,9},{9,17},{17,25},{2,10},{10,18},{18,26},{... | collective-permute-start | bytes 24584 | tf_op jit(solution)/shard_map/ppermute | solution.py:16
  10.4 1.3 collective-permute-start
  11.7 1.2 fusion.25
  12.9 1.0 fusion.24
  14.0 1.0 constant_dynamic-update-slice_fusion.1
  15.7 3.7 %collective-permute-start.3 = (f32[34,1,512]{2,1,0:T(1,128)S(1)}, f32[34,1,512]{2,1,0:T(1,128)S(1)}, u32[]{:S(2)}, u32[]{:S(2)}) collective-permute-start(f32[34,1,512]{2,1,0:T(1,128)S(1)} %get-tuple-element.12), channel_id=1, source_target_pairs={{0,1},{1,2},{2,3},{3,4},{4,5},{5,6},{6,7},{8,9},{9,10},{10,11},{11... | collective-permute-start | bytes 208904 | tf_op jit(solution)/shard_map/ppermute | solution.py:16
  19.4 1.3 collective-permute-start.2
  20.7 2.1 %fusion.15 = (f32[512,256]{1,0:T(8,128)S(1)}, f32[512,256]{1,0:T(8,128)S(1)}) fusion(), kind=kLoop, calls=%fused_computation.24 | loop fusion | flops 1835008 | bytes 1048576 | tf_op jit(solution)/shard_map/sin | solution.py:27
  22.7 2.8 %collective-permute-done.2 = f32[34,1,512]{2,1,0:T(1,128)S(1)} collective-permute-done((f32[34,1,512]{2,1,0:T(1,128)S(1)}, f32[34,1,512]{2,1,0:T(1,128)S(1)}, u32[]{:S(2)}, u32[]{:S(2)}) %collective-permute-start.2) | collective-permute-done | bytes 69664 | tf_op jit(solution)/shard_map/ppermute | solution.py:17
  25.6 1.2 multiply_reduce_fusion
  26.7 44.3 %all-reduce = (f32[]{:T(128)}, f32[]{:T(128)}) all-reduce(f32[]{:T(128)} %get-tuple-element.5, f32[]{:T(128)} %get-tuple-element.4), channel_id=1, replica_groups=mesh['radial'=4,'lateral'=8] {'radial','lateral'}, use_global_device_ids=true, to_apply=%region_1.2 | all-reduce | flops 2 | bytes 16 | tf_op jit(solution)/shard_map/psum | solution.py:35
  72.4 1.0 subtract_convert_fusion
  74.4 1.2 copy.20
  75.6 5.3 %all-to-all-start = ((bf16[4,256,256]{2,0,1:T(4,128)(2,1)}), bf16[4,256,256]{2,0,1:T(4,128)(2,1)S(1)}, u32[]{:S(2)}, u32[]{:S(2)}) async-start(bf16[4,256,256]{2,0,1:T(4,128)(2,1)} %copy.20), calls=%async_computation | async-start | bytes 1048576 | tf_op jit(solution)/shard_map/all_to_all | solution.py:50
  81.3 16.3 %all-to-all-done = bf16[4,256,256]{2,0,1:T(4,128)(2,1)S(1)} async-done(((bf16[4,256,256]{2,0,1:T(4,128)(2,1)}), bf16[4,256,256]{2,0,1:T(4,128)(2,1)S(1)}, u32[]{:S(2)}, u32[]{:S(2)}) %all-to-all-start) | async-done | bytes 524320 | tf_op jit(solution)/shard_map/all_to_all | solution.py:50
  97.7 3.0 %copy.26 = bf16[32,32,256,1]{1,0,3,2:T(8,128)(2,1)S(1)} copy(bf16[32,32,256,1]{2,1,0,3:T(8,128)(2,1)S(1)} %bitcast.23) | data formatting | bytes 1048576 | tf_op jit(solution)/shard_map/all_to_all | solution.py:50
  100.7 16.3 %all-gather.2.cloned.1.call-done = bf16[32,32,2,256]{3,0,2,1:T(8,128)(2,1)} async-done(((bf16[32,4,2,256]{3,0,2,1:T(8,128)(2,1)}), bf16[32,32,2,256]{3,0,2,1:T(8,128)(2,1)}) %all-gather.2.cloned.1.call-update) | async-done | bytes 1048592 | tf_op jit(solution)/shard_map/all_gather | solution.py:53
  117.0 7.2 %copy.23 = bf16[32,32,2,256]{0,1,2,3:T(8,128)(2,1)} copy(bf16[32,32,2,256]{3,0,2,1:T(8,128)(2,1)} %all-gather.2.cloned.1.call-done) | data formatting | bytes 2097152 | tf_op jit(solution)/shard_map/all_gather | solution.py:53
  124.2 6.7 %convolution_bitcast_fusion = f32[32,32,2,256]{0,1,2,3:T(8,128)} fusion(bf16[32,32,2,256]{0,1,2,3:T(8,128)(2,1)} %copy.23, bf16[32,32,256,1]{1,0,3,2:T(8,128)(2,1)S(1)} %copy.26), kind=kOutput, calls=%fused_computation | convolution fusion | flops 33554432 | bytes 3670016 | tf_op jit(solution)/shard_map/satm,alm->lstm/dot_general | solution.py:51
  130.9 7.1 %copy.25 = f32[32,32,2,256]{3,1,2,0:T(8,128)S(1)} copy(f32[32,32,2,256]{0,1,2,3:T(8,128)} %convolution_bitcast_fusion) | data formatting | bytes 4194304 | tf_op jit(solution)/shard_map/satm,alm->lstm/transpose | solution.py:51
  138.0 1.8 fusion.17
  139.8 30.3 %all-reduce.3.cloned.1.call-done = f32[32,2,2,256]{3,1,2,0:T(2,128)} async-done(((f32[32,2,2,256]{3,1,2,0:T(2,128)}), f32[32,2,2,256]{3,1,2,0:T(2,128)}) %all-reduce.3.cloned.1.call-update) | async-done | bytes 131088 | tf_op jit(solution)/shard_map/psum | solution.py:62
  170.1 1.1 fusion.26
  (34 shorter events, 3.6 us)
Async XLA Ops:
  7.2 74.0 %copy-start = (f32[2,32,256]{2,1,0:T(8,128)S(1)}, f32[2,32,256]{2,1,0:T(8,128)}, u32[]{:S(2)}) copy-start(f32[2,32,256]{2,1,0:T(8,128)} %param.13) | copy-start | bytes 196612
  7.2 18.4 %copy-start.1 = (f32[32,4,512]{2,1,0:T(4,128)S(1)}, f32[32,4,512]{2,1,0:T(4,128)}, u32[]{:S(2)}) copy-start(f32[32,4,512]{2,1,0:T(4,128)} %param.8) | copy-start | bytes 786436
  7.2 18.4 %copy-start.3 = (f32[32,4,512]{2,1,0:T(4,128)S(1)}, f32[32,4,512]{2,1,0:T(4,128)}, u32[]{:S(2)}) copy-start(f32[32,4,512]{2,1,0:T(4,128)} %param.9) | copy-start | bytes 786436
  7.2 109.8 %all-gather.2.cloned.1.call-start = ((), (), s32[]{:S(2)}) async-start(), calls=%async_computation.1 | async-start | bytes 1179648 | tf_op jit(solution)/shard_map/all_gather | solution.py:53
  8.0 6.0 %collective-permute-start.1 = (f32[1,4,512]{2,1,0:T(4,128)S(1)}, f32[1,4,512]{2,1,0:T(4,128)S(1)}, u32[]{:S(2)}, u32[]{:S(2)}) collective-permute-start(f32[1,4,512]{2,1,0:T(4,128)S(1)} %get-tuple-element.15), channel_id=1, source_target_pairs={{0,8},{8,16},{16,24},{1,9},{9,17},{17,25},{2,10},{10,18},{18,26},{... | collective-permute-start | bytes 24584 | tf_op jit(solution)/shard_map/ppermute | solution.py:16
  10.4 5.2 %collective-permute-start = (f32[1,4,512]{2,1,0:T(4,128)S(1)}, f32[1,4,512]{2,1,0:T(4,128)S(1)}, u32[]{:S(2)}, u32[]{:S(2)}) collective-permute-start(f32[1,4,512]{2,1,0:T(4,128)S(1)} %get-tuple-element.14), channel_id=1, source_target_pairs={{8,0},{16,8},{24,16},{9,1},{17,9},{25,17},{10,2},{18,10},{26,18},{... | collective-permute-start | bytes 24584 | tf_op jit(solution)/shard_map/ppermute | solution.py:17
  12.9 59.4 %copy-start.4 = (f32[32,4,512]{2,1,0:T(4,128)S(1)}, f32[32,4,512]{2,1,0:T(4,128)}, u32[]{:S(2)}) copy-start(f32[32,4,512]{2,1,0:T(4,128)} %param.10) | copy-start | bytes 786436
  12.9 59.4 %copy-start.5 = (f32[32,4,512]{2,1,0:T(4,128)S(1)}, f32[32,4,512]{2,1,0:T(4,128)}, u32[]{:S(2)}) copy-start(f32[32,4,512]{2,1,0:T(4,128)} %param.7) | copy-start | bytes 786436
  12.9 59.4 %copy-start.6 = (f32[32]{0:T(128)S(1)}, f32[32]{0:T(128)}, u32[]{:S(2)}) copy-start(f32[32]{0:T(128)} %param.11) | copy-start | bytes 388
  15.7 7.0 %collective-permute-start.3 = (f32[34,1,512]{2,1,0:T(1,128)S(1)}, f32[34,1,512]{2,1,0:T(1,128)S(1)}, u32[]{:S(2)}, u32[]{:S(2)}) collective-permute-start(f32[34,1,512]{2,1,0:T(1,128)S(1)} %get-tuple-element.12), channel_id=1, source_target_pairs={{0,1},{1,2},{2,3},{3,4},{4,5},{5,6},{6,7},{8,9},{9,10},{10,11},{11... | collective-permute-start | bytes 208904 | tf_op jit(solution)/shard_map/ppermute | solution.py:16
  19.4 6.2 %collective-permute-start.2 = (f32[34,1,512]{2,1,0:T(1,128)S(1)}, f32[34,1,512]{2,1,0:T(1,128)S(1)}, u32[]{:S(2)}, u32[]{:S(2)}) collective-permute-start(f32[34,1,512]{2,1,0:T(1,128)S(1)} %get-tuple-element.11), channel_id=1, source_target_pairs={{1,0},{2,1},{3,2},{4,3},{5,4},{6,5},{7,6},{9,8},{10,9},{11,10},{12... | collective-permute-start | bytes 208904 | tf_op jit(solution)/shard_map/ppermute | solution.py:17
  26.7 47.6 %copy-start.2 = (bf16[4,256,256]{2,1,0:T(8,128)(2,1)S(1)}, bf16[4,256,256]{2,1,0:T(8,128)(2,1)}, u32[]{:S(2)}) copy-start(bf16[4,256,256]{2,1,0:T(8,128)(2,1)} %param.12) | copy-start | bytes 1572868
  75.6 21.9 %all-to-all-start = ((bf16[4,256,256]{2,0,1:T(4,128)(2,1)}), bf16[4,256,256]{2,0,1:T(4,128)(2,1)S(1)}, u32[]{:S(2)}, u32[]{:S(2)}) async-start(bf16[4,256,256]{2,0,1:T(4,128)(2,1)} %copy.20), calls=%async_computation | async-start | bytes 1048576 | tf_op jit(solution)/shard_map/all_to_all | solution.py:50
  80.9 89.2 %all-reduce.3.cloned.1.call-start = ((), (), s32[]{:S(2)}) async-start(), calls=%async_computation.2 | async-start | bytes 262144 | tf_op jit(solution)/shard_map/psum | solution.py:62
Sparse Core Ops, SparseCore 0:
  74.5 42.4 all-gather.1
  139.9 30.1 all-reduce.2
where the time goes:
time: 180 us; the launch traced here: 179 us
  waiting for transfers between devices  66.3 us (37%)
  blocking collectives  44.3 us (25%)
  local copies, waits for them, and re-layouts  26.1 us (14%)
  between operations  15.6 us (9%)
  starting transfers between devices  14.1 us (8%)
  matrix products  8.74 us (5%)
  other arithmetic  4.2 us (2%)
    psum x1, blocking collectives, on_device(): lax.psum((jnp.sum(residual * residual), jnp.sum(residual * image)), ('rad...  44.3 us
    psum x1, waiting for transfers between devices, on_device(): response = lax.psum(partial_terms, 'radial')  30.3 us
    all_gather x1, waiting for transfers between devices, on_device(): lax.all_gather(spectrum, 'lateral', axis=1, tiled=True)  16.3 us
    all_to_all x1, waiting for transfers between devices, on_device(): lax.all_to_all(legendre, 'lateral', split_axis=1, concat_axis=0, tiled=True)  16.3 us
    all_gather x1, local copies, waits for them, and re-layouts, on_device(): lax.all_gather(spectrum, 'lateral', axis=1, tiled=True)  7.21 us
    transpose x1, local copies, waits for them, and re-layouts, on_device(): jnp.einsum('satm,alm->lstm', lax.all_gather(spectrum, 'lateral', axis=1,...  7.08 us
    dot_general x1, matrix products, on_device(): jnp.einsum('satm,alm->lstm', lax.all_gather(spectrum, 'lateral', axis=1,...  6.72 us
    ppermute x2, starting transfers between devices, padded_2(): before = lax.ppermute(last, axis, up)  6 us
  transfers between devices with their start and end apart: 7, of which 5 were waited for; matrix products, arithmetic and copies ran while one was open for 5% of the time, Pallas kernels for 0%

commit v1 on v0

v1 whole, which is shorter than its diff:
```python
import functools
import math

import jax
import jax.numpy as jnp
import numpy as np
from jax import lax
from jax.experimental import pallas as pl
from jax.experimental.pallas import tpu as pltpu
from jax.sharding import PartitionSpec as P

MESH = pl.DeviceIdType.MESH
F32 = jnp.float32
BF16 = jnp.bfloat16


def fourier_table(nlon, orders):
    column = np.arange(nlon, dtype=np.int32)[:, None]
    order = np.arange(orders, dtype=np.int32)[None, :]
    phase = np.float32(2.0 * math.pi / nlon) * (column * order % nlon).astype(np.float32)
    scale = np.float32(1.0 / math.sqrt(nlon))
    return (np.concatenate([np.cos(phase), np.sin(phase)], axis=1) * scale).astype(BF16)


def send(src, dst, send_sem, recv_sem, axis, target):
    copy = pltpu.make_async_remote_copy(
        src_ref=src,
        dst_ref=dst,
        send_sem=send_sem,
        recv_sem=recv_sem,
        device_id={axis: target},
        device_id_type=MESH,
    )
    copy.start()
    return copy


def folded(x):
    rows = x.shape[0] // 8
    cols = x.shape[1] // 128
    total = None
    for i in range(rows):
        for j in range(cols):
            part = x[i * 8 : (i + 1) * 8, j * 128 : (j + 1) * 128]
            total = part if total is None else total + part
    return total


def kernel(
    nr, nl,
    pres, res, visc, therm, comp, leg, ker, table,
    pres_out, res_out, final,
    shell_send, shell_recv, cycle_send, cycle_recv,
    dot_r, dot_l, spec_send, spec_recv, ker_recv, ker_t, part, wire, terms,
    shell_ss, shell_rs, cycle_ss, cycle_rs,
    dotr_ss, dotr_rs, dotl_ss, dotl_rs,
    spec_ss, spec_rs, ker_ss, ker_rs, term_ss, term_rs, fin_ss, fin_rs,
):
    ri, li = lax.axis_index("radial"), lax.axis_index("lateral")
    shells, cycles, nlon = res.shape
    degrees = leg.shape[1]
    orders = leg.shape[2]
    owned = degrees // nl
    block = table.shape[1] // nr

    barrier = pltpu.get_barrier_semaphore()
    for d in range(1, nr):
        pl.semaphore_signal(barrier, inc=1, device_id={"radial": lax.rem(ri + d, nr)}, device_id_type=MESH)
    for d in range(1, nl):
        pl.semaphore_signal(barrier, inc=1, device_id={"lateral": lax.rem(li + d, nl)}, device_id_type=MESH)

    r = [res[:, a, :] for a in range(cycles)]
    for a in range(cycles):
        shell_send[0, a : a + 1, :] = r[a][0:1]
        shell_send[1, a : a + 1, :] = r[a][shells - 1 : shells]
    cycle_send[0] = r[0]
    cycle_send[1] = r[cycles - 1]
    pl.semaphore_wait(barrier, nr - 1 + nl - 1)

    def edge(sender, receiver, ss, rs, slot, axis, target):
        return pltpu.make_async_remote_copy(
            src_ref=sender.at[slot], dst_ref=receiver.at[slot],
            send_sem=ss.at[slot], recv_sem=rs.at[slot],
            device_id={axis: target}, device_id_type=MESH,
        )

    sides = (
        (cycle_send, cycle_recv, cycle_ss, cycle_rs, "lateral", li, nl),
        (shell_send, shell_recv, shell_ss, shell_rs, "radial", ri, nr),
    )
    for sender, receiver, ss, rs, axis, me, n in sides:
        @pl.when(me > 0)
        def _():
            edge(sender, receiver, ss, rs, 0, axis, lax.rem(me + n - 1, n)).start()

        @pl.when(me < n - 1)
        def _():
            edge(sender, receiver, ss, rs, 1, axis, lax.rem(me + 1, n)).start()

    later = []
    ker_copies = []
    for d in range(1, nr):
        ker_copies.append(send(ker, ker_recv.at[d], ker_ss.at[d], ker_rs.at[d], "radial", lax.rem(ri + d, nr)))

    rows = lax.broadcasted_iota(jnp.int32, (shells, shells), 0)
    lanes = lax.broadcasted_iota(jnp.int32, (shells, shells), 1)
    spread = jnp.broadcast_to(comp[...], (shells, shells))
    scale = jnp.sum(jnp.where(rows == lanes, spread, 0.0), axis=1, keepdims=True)
    row = lax.broadcasted_iota(jnp.int32, (shells, nlon), 0)
    squares = None
    for a in range(cycles):
        term = folded(r[a] * r[a])
        squares = term if squares is None else squares + term

    for sender, receiver, ss, rs, axis, me, n in sides:
        @pl.when(me < n - 1)
        def _():
            edge(sender, receiver, ss, rs, 0, axis, lax.rem(me + 1, n)).wait_recv()

        @pl.when(me == n - 1)
        def _():
            receiver[0] = jnp.zeros(receiver.shape[1:], F32)

        @pl.when(me > 0)
        def _():
            edge(sender, receiver, ss, rs, 1, axis, lax.rem(me + n - 1, n)).wait_recv()

        @pl.when(me == 0)
        def _():
            receiver[1] = jnp.zeros(receiver.shape[1:], F32)

    image = []
    curvature = None
    for a in range(cycles):
        x = r[a]
        up = jnp.where(row == shells - 1, shell_recv[0, a : a + 1, :], pltpu.roll(x, shells - 1, 0))
        down = jnp.where(row == 0, shell_recv[1, a : a + 1, :], pltpu.roll(x, 1, 0))
        following = r[a + 1] if a + 1 < cycles else cycle_recv[0]
        preceding = r[a - 1] if a > 0 else cycle_recv[1]
        beside = up + down + following + preceding
        beside = beside + pltpu.roll(x, 1, 1) + pltpu.roll(x, nlon - 1, 1)
        y = (6.0 + visc[:, a, :]) * x - beside
        image.append(y)
        term = folded(x * y)
        curvature = term if curvature is None else curvature + term

    dot_r[0, 0:8] = squares
    dot_r[0, 8:16] = curvature
    copies = [
        send(dot_r.at[0], dot_r.at[d], dotr_ss.at[d], dotr_rs.at[d], "radial", lax.rem(ri + d, nr))
        for d in range(1, nr)
    ]
    later += copies
    ker_recv[0] = ker[...]
    for copy in ker_copies:
        copy.wait_recv()
    later += ker_copies
    for k in range(2):
        whole = jnp.concatenate([ker_recv[d, k] for d in range(nr)], axis=0).T
        high = whole.astype(BF16)
        ker_t[k, :, 0 : nr * shells] = high
        ker_t[k, :, nr * shells :] = (whole - high.astype(F32)).astype(BF16)
    for copy in copies:
        copy.wait_recv()
    total = dot_r[0]
    for d in range(1, nr):
        total = total + dot_r[d]
    dot_l[0] = total
    copies = [
        send(dot_l.at[0], dot_l.at[d], dotl_ss.at[d], dotl_rs.at[d], "lateral", lax.rem(li + d, nl))
        for d in range(1, nl)
    ]
    later += copies
    for copy in copies:
        copy.wait_recv()
    total = dot_l[0]
    for d in range(1, nl):
        total = total + dot_l[d]
    alpha = jnp.sum(total[0:8], keepdims=True) / jnp.sum(total[8:16], keepdims=True)

    anomaly = []
    for a in range(cycles):
        new = pres[:, a, :] + alpha * r[a]
        pres_out[a] = new
        anomaly.append((therm[:, a, :] - scale * new).astype(BF16))
    spectrum = jnp.dot(jnp.concatenate(anomaly, axis=0), table[...], preferred_element_type=F32).astype(BF16)
    for b in range(nr):
        for a in range(cycles):
            spec_send[b, :, a * block : (a + 1) * block] = spectrum[
                a * shells : (a + 1) * shells, b * block : (b + 1) * block
            ]
    copies = []
    for d in range(1, nr):
        target = lax.rem(ri + d, nr)
        copies.append(send(spec_send.at[target], spec_recv.at[d], spec_ss.at[d], spec_rs.at[d], "radial", target))
    later += copies
    spec_recv[0] = spec_send[ri]
    for a in range(cycles):
        res_out[a] = r[a] - alpha * image[a]
    for copy in copies:
        copy.wait_recv()

    stack = jnp.concatenate([spec_recv[d] for d in range(nr)], axis=0)
    stack = jnp.concatenate([stack, stack], axis=0)
    first = pl.multiple_of(lax.rem(ri * block, orders), block)
    for k in range(2):
        weighted = jnp.dot(ker_t[k], stack, preferred_element_type=F32)
        value = None
        for a in range(cycles):
            term = weighted[:, a * block : (a + 1) * block] * leg[a, :, pl.ds(first, block)].astype(F32)
            value = term if value is None else value + term
        for b in range(nl):
            piece = value[b * owned : (b + 1) * owned]
            part[b, k * owned : (k + 1) * owned, :] = piece
            wire[b, k * owned : (k + 1) * owned, :] = piece.astype(wire.dtype)
    copies = []
    for d in range(1, nl):
        target = lax.rem(li + d, nl)
        copies.append(send(wire.at[target], terms.at[d], term_ss.at[d], term_rs.at[d], "lateral", target))
    later += copies
    total = part[li]
    for d in range(1, nl):
        copies[d - 1].wait_recv()
        total = total + terms[d].astype(F32)
    mine = pl.ds(pl.multiple_of(ri * block, block), block)
    for k in range(2):
        final[k, :, mine] = total[k * owned : (k + 1) * owned]
    copies = [
        send(final.at[:, :, mine], final.at[:, :, mine], fin_ss.at[d], fin_rs.at[d], "radial", lax.rem(ri + d, nr))
        for d in range(1, nr)
    ]
    for d in range(1, nr):
        origin = lax.rem(ri + nr - d, nr)
        theirs = pl.ds(pl.multiple_of(origin * block, block), block)
        pltpu.make_async_remote_copy(
            src_ref=final.at[:, :, theirs], dst_ref=final.at[:, :, theirs],
            send_sem=fin_ss.at[d], recv_sem=fin_rs.at[d],
            device_id={"radial": origin}, device_id_type=MESH,
        ).wait_recv()
    for copy in later + copies:
        copy.wait_send()
    for sender, receiver, ss, rs, axis, me, n in sides:
        @pl.when(me > 0)
        def _():
            edge(sender, receiver, ss, rs, 0, axis, lax.rem(me + n - 1, n)).wait_send()

        @pl.when(me < n - 1)
        def _():
            edge(sender, receiver, ss, rs, 1, axis, lax.rem(me + 1, n)).wait_send()


def on_device(pressure, residual, inv_visc, thermal, compress, legendre, kernels):
    nr, nl = lax.axis_size("radial"), lax.axis_size("lateral")
    shells, cycles, nlon = residual.shape
    degrees, orders = legendre.shape[1:]
    owned = degrees // nl
    block = 2 * orders // nr
    wire = BF16 if owned % 16 == 0 else F32
    table = jnp.asarray(fourier_table(nlon, orders))
    dma = pltpu.SemaphoreType.DMA
    vmem = pl.BlockSpec(memory_space=pltpu.VMEM)
    pressure_new, residual_new, response = pl.pallas_call(
        functools.partial(kernel, nr, nl),
        out_shape=(
            jax.ShapeDtypeStruct((cycles, shells, nlon), F32),
            jax.ShapeDtypeStruct((cycles, shells, nlon), F32),
            jax.ShapeDtypeStruct((2, owned, 2 * orders), F32),
        ),
        in_specs=[vmem] * 8,
        out_specs=(vmem,) * 3,
        scratch_shapes=[
            pltpu.VMEM((2, cycles, nlon), F32),
            pltpu.VMEM((2, cycles, nlon), F32),
            pltpu.VMEM((2, shells, nlon), F32),
            pltpu.VMEM((2, shells, nlon), F32),
            pltpu.VMEM((nr, 16, 128), F32),
            pltpu.VMEM((nl, 16, 128), F32),
            pltpu.VMEM((nr, shells, cycles * block), BF16),
            pltpu.VMEM((nr, shells, cycles * block), BF16),
            pltpu.VMEM((nr, 2, shells, degrees), F32),
            pltpu.VMEM((2, degrees, 2 * nr * shells), BF16),
            pltpu.VMEM((nl, 2 * owned, block), F32),
            pltpu.VMEM((nl, 2 * owned, block), wire),
            pltpu.VMEM((nl, 2 * owned, block), wire),
            dma((2,)), dma((2,)), dma((2,)), dma((2,)),
            dma((nr,)), dma((nr,)), dma((nl,)), dma((nl,)),
            dma((nr,)), dma((nr,)), dma((nr,)), dma((nr,)),
            dma((nl,)), dma((nl,)), dma((nr,)), dma((nr,)),
        ],
        compiler_params=pltpu.CompilerParams(
            collective_id=0, has_side_effects=True, vmem_limit_bytes=40 * 2**20
        ),
    )(pressure, residual, inv_visc, thermal, compress[None, :], legendre, kernels, table)
    response = response.reshape(2, owned, 2, orders)
    return (
        jnp.transpose(pressure_new, (1, 0, 2)),
        jnp.transpose(residual_new, (1, 0, 2)),
        response[0],
        response[1],
    )


def solution(mesh):
    return jax.shard_map(
        on_device,
        mesh=mesh,
        in_specs=(
            P("radial", "lateral", None),
            P("radial", "lateral", None),
            P("radial", "lateral", None),
            P("radial", "lateral", None),
            P("radial"),
            P("lateral", None, None),
            P(None, "radial", None),
        ),
        out_specs=(
            P("radial", "lateral", None),
            P("radial", "lateral", None),
            P("lateral", None, None),
            P("lateral", None, None),
        ),
        check_vma=False,
    )
```

time: 180 us -> 40.6 us (0.23)
  waiting for transfers between devices: 66.3 us -> 0 us
  blocking collectives: 44.3 us -> 0 us
  Pallas kernels: 0 us -> 29.1 us
  local copies, waits for them, and re-layouts: 26.1 us -> 10.5 us
  between operations: 15.6 us -> 0.66 us
  starting transfers between devices: 14.1 us -> 0 us
  matrix products: 8.74 us -> 0 us
  other arithmetic: 4.2 us -> 0 us
    psum x1 -> x0, blocking collectives: 44.3 us -> none  [on_device(): lax.psum((jnp.sum(residual * residual), jnp.sum(residual * image)), ('rad...]
    psum x1 -> x0, waiting for transfers between devices: 30.3 us -> none  [on_device(): response = lax.psum(partial_terms, 'radial')]
    pallas_call x0 -> x1, Pallas kernels: none -> 29.1 us  [on_device(): pl.pallas_call(functools.partial(kernel, nr, nl), out_shape=(jax.ShapeDty...]
    all_gather x1 -> x0, waiting for transfers between devices: 16.3 us -> none  [on_device(): lax.all_gather(spectrum, 'lateral', axis=1, tiled=True)]
    all_to_all x1 -> x0, waiting for transfers between devices: 16.3 us -> none  [on_device(): lax.all_to_all(legendre, 'lateral', split_axis=1, concat_axis=0, tiled=True)]
    dot_general x3 -> x0, matrix products: 8.74 us -> none  [the longest x1 6.72 us: on_device(): jnp.einsum('satm,alm->lstm', lax.all_gather(spectrum, 'lateral', axis=1,...]
    ppermute x4 -> x0, starting transfers between devices: 8.58 us -> none  [the longest x2 6 us: padded_2(): before = lax.ppermute(last, axis, up)]
    all_gather x1 -> x0, local copies, waits for them, and re-layouts: 7.21 us -> none  [on_device(): lax.all_gather(spectrum, 'lateral', axis=1, tiled=True)]
  transfers between devices with their start and end apart: 7 -> 0, of which waited for: 5 -> 0; matrix products, arithmetic and copies ran while one was open for 5% -> 0% of each run, Pallas kernels for 0% -> 0%
where the time goes in v1:
time: 40.6 us; the launch traced here: 40.2 us
  Pallas kernels  29.1 us (72%)
  local copies, waits for them, and re-layouts  10.5 us (26%)
  between operations  0.66 us (2%)
    pallas_call x1, Pallas kernels, on_device(): pl.pallas_call(functools.partial(kernel, nr, nl), out_shape=(jax.ShapeDty...  29.1 us
    unnamed x18, local copies, waits for them, and re-layouts  9.11 us

profile of v1, /device:TPU:0, one launch (start us, length us, event | category | flops | bytes accessed | tf_op | source)
XLA Modules:
  0.0 40.2 jit_solution(9971772893897059537)
XLA Ops:
  0.6 0.0 copy-start.7
  0.6 0.6 %copy-done.7 = f32[32]{0:T(128)S(1)} copy-done((f32[32]{0:T(128)S(1)}, f32[32]{0:T(128)}, u32[]{:S(2)}) %copy-start.7) | copy-done | bytes 152
  1.3 0.0 copy-start
  1.3 1.0 %copy-done = bf16[4,256,256]{2,1,0:T(8,128)(2,1)S(1)} copy-done((bf16[4,256,256]{2,1,0:T(8,128)(2,1)S(1)}, bf16[4,256,256]{2,1,0:T(8,128)(2,1)}, u32[]{:S(2)}) %copy-start) | copy-done | bytes 524312
  2.3 0.0 copy-start.1
  2.3 1.0 %copy-done.1 = bf16[512,512]{1,0:T(8,128)(2,1)S(1)} copy-done((bf16[512,512]{1,0:T(8,128)(2,1)S(1)}, bf16[512,512]{1,0:T(8,128)(2,1)}, u32[]{:S(2)}) %copy-start.1) | copy-done | bytes 524312
  3.4 0.0 copy-start.2
  3.4 0.9 %copy-done.2 = f32[32,4,512]{2,1,0:T(4,128)S(1)} copy-done((f32[32,4,512]{2,1,0:T(4,128)S(1)}, f32[32,4,512]{2,1,0:T(4,128)}, u32[]{:S(2)}) %copy-start.2) | copy-done | bytes 262168
  4.3 0.0 copy-start.3
  4.3 0.9 %copy-done.3 = f32[32,4,512]{2,1,0:T(4,128)S(1)} copy-done((f32[32,4,512]{2,1,0:T(4,128)S(1)}, f32[32,4,512]{2,1,0:T(4,128)}, u32[]{:S(2)}) %copy-start.3) | copy-done | bytes 262168
  5.3 0.0 copy-start.4
  5.3 0.9 %copy-done.4 = f32[32,4,512]{2,1,0:T(4,128)S(1)} copy-done((f32[32,4,512]{2,1,0:T(4,128)S(1)}, f32[32,4,512]{2,1,0:T(4,128)}, u32[]{:S(2)}) %copy-start.4) | copy-done | bytes 262168
  6.2 0.0 copy-start.5
  6.2 0.9 %copy-done.5 = f32[32,4,512]{2,1,0:T(4,128)S(1)} copy-done((f32[32,4,512]{2,1,0:T(4,128)S(1)}, f32[32,4,512]{2,1,0:T(4,128)}, u32[]{:S(2)}) %copy-start.5) | copy-done | bytes 262168
  7.2 0.0 copy-start.6
  7.2 0.8 %copy-done.6 = f32[2,32,256]{2,1,0:T(8,128)S(1)} copy-done((f32[2,32,256]{2,1,0:T(8,128)S(1)}, f32[2,32,256]{2,1,0:T(8,128)}, u32[]{:S(2)}) %copy-start.6) | copy-done | bytes 65560
  8.0 29.1 %shard_map.111 = (f32[4,32,512]{2,1,0:T(8,128)S(1)}, f32[4,32,512]{2,1,0:T(8,128)S(1)}, f32[2,32,512]{2,1,0:T(8,128)S(1)}) custom-call(f32[32,4,512]{2,1,0:T(4,128)S(1)} %copy-done.2, f32[32,4,512]{2,1,0:T(4,128)S(1)} %copy-done.3, f32[32,4,512]{2,1,0:T(4,128)S(1)} %copy-done.4, f32[32,4,512]{2,1,0:T(4,128)S(1)} %copy-done.5, f32[1,32]{1,0:T(1,128)S(1)} %bitcast.5, ...), custom_call_target="tpu_custom_call" | custom-call | tf_op jit(solution)/shard_map/pallas_call | solution.py:262
  37.1 0.9 %copy.12 = f32[32,4,512]{2,1,0:T(4,128)} copy(f32[32,4,512]{2,0,1:T(8,128)S(1)} %bitcast.4) | data formatting | bytes 524288
  38.0 0.9 %copy.13 = f32[32,4,512]{2,1,0:T(4,128)} copy(f32[32,4,512]{2,0,1:T(8,128)S(1)} %bitcast.3) | data formatting | bytes 524288
  38.9 0.7 %squeeze.7 = f32[32,2,256]{2,1,0:T(2,128)} reshape(f32[1,32,512]{2,1,0:T(8,128)S(1)} %get-tuple-element.14) | data formatting | bytes 131072 | tf_op jit(solution)/shard_map/squeeze | solution.py:299
  39.6 0.7 %squeeze.6 = f32[32,2,256]{2,1,0:T(2,128)} reshape(f32[1,32,512]{2,1,0:T(8,128)S(1)} %get-tuple-element.15) | data formatting | bytes 131072 | tf_op jit(solution)/shard_map/squeeze | solution.py:298
  (1 shorter events, 0.0 us)
Async XLA Ops:
  0.6 0.7 %copy-start.7 = (f32[32]{0:T(128)S(1)}, f32[32]{0:T(128)}, u32[]{:S(2)}) copy-start(f32[32]{0:T(128)} %param.12) | copy-start | bytes 388
  1.3 1.0 %copy-start = (bf16[4,256,256]{2,1,0:T(8,128)(2,1)S(1)}, bf16[4,256,256]{2,1,0:T(8,128)(2,1)}, u32[]{:S(2)}) copy-start(bf16[4,256,256]{2,1,0:T(8,128)(2,1)} %leg.1) | copy-start | bytes 1572868
  2.3 1.0 %copy-start.1 = (bf16[512,512]{1,0:T(8,128)(2,1)S(1)}, bf16[512,512]{1,0:T(8,128)(2,1)}, u32[]{:S(2)}) copy-start(bf16[512,512]{1,0:T(8,128)(2,1)} %constant.2.clone.table) | copy-start | bytes 1572868
  3.4 0.9 %copy-start.2 = (f32[32,4,512]{2,1,0:T(4,128)S(1)}, f32[32,4,512]{2,1,0:T(4,128)}, u32[]{:S(2)}) copy-start(f32[32,4,512]{2,1,0:T(4,128)} %pres.1) | copy-start | bytes 786436
  4.3 0.9 %copy-start.3 = (f32[32,4,512]{2,1,0:T(4,128)S(1)}, f32[32,4,512]{2,1,0:T(4,128)}, u32[]{:S(2)}) copy-start(f32[32,4,512]{2,1,0:T(4,128)} %res.1) | copy-start | bytes 786436
  5.3 0.9 %copy-start.4 = (f32[32,4,512]{2,1,0:T(4,128)S(1)}, f32[32,4,512]{2,1,0:T(4,128)}, u32[]{:S(2)}) copy-start(f32[32,4,512]{2,1,0:T(4,128)} %visc.1) | copy-start | bytes 786436
  6.2 0.9 %copy-start.5 = (f32[32,4,512]{2,1,0:T(4,128)S(1)}, f32[32,4,512]{2,1,0:T(4,128)}, u32[]{:S(2)}) copy-start(f32[32,4,512]{2,1,0:T(4,128)} %therm.1) | copy-start | bytes 786436
  7.2 0.8 %copy-start.6 = (f32[2,32,256]{2,1,0:T(8,128)S(1)}, f32[2,32,256]{2,1,0:T(8,128)}, u32[]{:S(2)}) copy-start(f32[2,32,256]{2,1,0:T(8,128)} %ker.1) | copy-start | bytes 196612

commit v2 on v1

--- a/solution.py
+++ b/solution.py
@@ -48,8 +48,10 @@
 
 def kernel(
     nr, nl,
-    pres, res, visc, therm, comp, leg, ker, table,
-    pres_out, res_out, final,
+    pres_hbm, res_hbm, visc_hbm, therm_hbm, comp_hbm, leg_hbm, ker_hbm, table_hbm,
+    pres_hbm_out, res_hbm_out, geoid_hbm_out, topo_hbm_out,
+    pres, res, visc, therm, comp, leg, ker, table, load_sem, final,
+    pres_out, res_out, geoid_out, topo_out, store_sem,
     shell_send, shell_recv, cycle_send, cycle_recv,
     dot_r, dot_l, spec_send, spec_recv, ker_recv, ker_t, part, wire, terms,
     shell_ss, shell_rs, cycle_ss, cycle_rs,
@@ -63,12 +65,21 @@
     owned = degrees // nl
     block = table.shape[1] // nr
 
+    loads = {}
+    sources = (res_hbm, visc_hbm, comp_hbm, ker_hbm, pres_hbm, therm_hbm, table_hbm, leg_hbm)
+    targets = (res, visc, comp, ker, pres, therm, table, leg)
+    names = ("res", "visc", "comp", "ker", "pres", "therm", "table", "leg")
+    for i, (name, source, target) in enumerate(zip(names, sources, targets)):
+        loads[name] = pltpu.make_async_copy(source, target, load_sem.at[i])
+        loads[name].start()
+
     barrier = pltpu.get_barrier_semaphore()
     for d in range(1, nr):
         pl.semaphore_signal(barrier, inc=1, device_id={"radial": lax.rem(ri + d, nr)}, device_id_type=MESH)
     for d in range(1, nl):
         pl.semaphore_signal(barrier, inc=1, device_id={"lateral": lax.rem(li + d, nl)}, device_id_type=MESH)
 
+    loads["res"].wait()
     r = [res[:, a, :] for a in range(cycles)]
     for a in range(cycles):
         shell_send[0, a : a + 1, :] = r[a][0:1]
@@ -98,9 +109,10 @@
             edge(sender, receiver, ss, rs, 1, axis, lax.rem(me + 1, n)).start()
 
     later = []
-    ker_copies = []
-    for d in range(1, nr):
-        ker_copies.append(send(ker, ker_recv.at[d], ker_ss.at[d], ker_rs.at[d], "radial", lax.rem(ri + d, nr)))
+    loads["ker"].wait()
+    ker_recv[0] = ker[...].astype(BF16)
+    loads["comp"].wait()
+    loads["visc"].wait()
 
     rows = lax.broadcasted_iota(jnp.int32, (shells, shells), 0)
     lanes = lax.broadcasted_iota(jnp.int32, (shells, shells), 1)
@@ -151,15 +163,13 @@
         for d in range(1, nr)
     ]
     later += copies
-    ker_recv[0] = ker[...]
-    for copy in ker_copies:
-        copy.wait_recv()
+    ker_copies = [
+        send(ker_recv.at[0], ker_recv.at[d], ker_ss.at[d], ker_rs.at[d], "radial", lax.rem(ri + d, nr))
+        for d in range(1, nr)
+    ]
     later += ker_copies
-    for k in range(2):
-        whole = jnp.concatenate([ker_recv[d, k] for d in range(nr)], axis=0).T
-        high = whole.astype(BF16)
-        ker_t[k, :, 0 : nr * shells] = high
-        ker_t[k, :, nr * shells :] = (whole - high.astype(F32)).astype(BF16)
+    for name in ("pres", "therm", "table", "leg"):
+        loads[name].wait()
     for copy in copies:
         copy.wait_recv()
     total = dot_r[0]
@@ -178,10 +188,10 @@
         total = total + dot_l[d]
     alpha = jnp.sum(total[0:8], keepdims=True) / jnp.sum(total[8:16], keepdims=True)
 
-    anomaly = []
+    anomaly, pressure_new = [], []
     for a in range(cycles):
         new = pres[:, a, :] + alpha * r[a]
-        pres_out[a] = new
+        pressure_new.append(new)
         anomaly.append((therm[:, a, :] - scale * new).astype(BF16))
     spectrum = jnp.dot(jnp.concatenate(anomaly, axis=0), table[...], preferred_element_type=F32).astype(BF16)
     for b in range(nr):
@@ -195,13 +205,15 @@
         copies.append(send(spec_send.at[target], spec_recv.at[d], spec_ss.at[d], spec_rs.at[d], "radial", target))
     later += copies
     spec_recv[0] = spec_send[ri]
-    for a in range(cycles):
-        res_out[a] = r[a] - alpha * image[a]
-    for copy in copies:
+    for copy in ker_copies:
         copy.wait_recv()
+    for k in range(2):
+        whole = jnp.concatenate([ker_recv[d, k].astype(F32) for d in range(nr)], axis=0)
+        ker_t[k] = whole.T.astype(BF16)
+    for copy in copies:
+        copy.wait_recv()
 
     stack = jnp.concatenate([spec_recv[d] for d in range(nr)], axis=0)
-    stack = jnp.concatenate([stack, stack], axis=0)
     first = pl.multiple_of(lax.rem(ri * block, orders), block)
     for k in range(2):
         weighted = jnp.dot(ker_t[k], stack, preferred_element_type=F32)
@@ -218,6 +230,15 @@
         target = lax.rem(li + d, nl)
         copies.append(send(wire.at[target], terms.at[d], term_ss.at[d], term_rs.at[d], "lateral", target))
     later += copies
+    for a in range(cycles):
+        pres_out[:, a, :] = pressure_new[a]
+        res_out[:, a, :] = r[a] - alpha * image[a]
+    stores = [
+        pltpu.make_async_copy(pres_out, pres_hbm_out, store_sem.at[0]),
+        pltpu.make_async_copy(res_out, res_hbm_out, store_sem.at[1]),
+    ]
+    for store in stores:
+        store.start()
     total = part[li]
     for d in range(1, nl):
         copies[d - 1].wait_recv()
@@ -237,8 +258,19 @@
             send_sem=fin_ss.at[d], recv_sem=fin_rs.at[d],
             device_id={"radial": origin}, device_id_type=MESH,
         ).wait_recv()
+    for c in range(2):
+        geoid_out[:, c, :] = final[0, :, c * orders : (c + 1) * orders]
+        topo_out[:, c, :] = final[1, :, c * orders : (c + 1) * orders]
+    responses = [
+        pltpu.make_async_copy(geoid_out, geoid_hbm_out, store_sem.at[2]),
+        pltpu.make_async_copy(topo_out, topo_hbm_out, store_sem.at[3]),
+    ]
+    for store in responses:
+        store.start()
     for copy in later + copies:
         copy.wait_send()
+    for store in stores + responses:
+        store.wait()
     for sender, receiver, ss, rs, axis, me, n in sides:
         @pl.when(me > 0)
         def _():
@@ -247,6 +279,15 @@
         @pl.when(me < n - 1)
         def _():
             edge(sender, receiver, ss, rs, 1, axis, lax.rem(me + 1, n)).wait_send()
+
+
+def placed(*refs):
+    sources, targets, sem = refs[:4], refs[4:8], refs[8]
+    copies = [pltpu.make_async_copy(a, b, sem.at[i]) for i, (a, b) in enumerate(zip(sources, targets))]
+    for copy in copies:
+        copy.start()
+    for copy in copies:
+        copy.wait()
 
 
 def on_device(pressure, residual, inv_visc, thermal, compress, legendre, kernels):
@@ -258,17 +299,25 @@
     wire = BF16 if owned % 16 == 0 else F32
     table = jnp.asarray(fourier_table(nlon, orders))
     dma = pltpu.SemaphoreType.DMA
-    vmem = pl.BlockSpec(memory_space=pltpu.VMEM)
-    pressure_new, residual_new, response = pl.pallas_call(
+    anywhere = pl.BlockSpec(memory_space=pl.ANY)
+    operands = (pressure, residual, inv_visc, thermal, compress[None, :], legendre, kernels, table)
+    outputs = (
+        jax.ShapeDtypeStruct(pressure.shape, F32),
+        jax.ShapeDtypeStruct(residual.shape, F32),
+        jax.ShapeDtypeStruct((owned, 2, orders), F32),
+        jax.ShapeDtypeStruct((owned, 2, orders), F32),
+    )
+    results = pl.pallas_call(
         functools.partial(kernel, nr, nl),
-        out_shape=(
-            jax.ShapeDtypeStruct((cycles, shells, nlon), F32),
-            jax.ShapeDtypeStruct((cycles, shells, nlon), F32),
-            jax.ShapeDtypeStruct((2, owned, 2 * orders), F32),
-        ),
-        in_specs=[vmem] * 8,
-        out_specs=(vmem,) * 3,
+        out_shape=outputs,
+        in_specs=[anywhere] * 8,
+        out_specs=(anywhere,) * 4,
         scratch_shapes=[
+            *(pltpu.VMEM(x.shape, x.dtype) for x in operands),
+            dma((8,)),
+            pltpu.VMEM((2, owned, 2 * orders), F32),
+            *(pltpu.VMEM(x.shape, x.dtype) for x in outputs),
+            dma((4,)),
             pltpu.VMEM((2, cycles, nlon), F32),
             pltpu.VMEM((2, cycles, nlon), F32),
             pltpu.VMEM((2, shells, nlon), F32),
@@ -277,8 +326,8 @@
             pltpu.VMEM((nl, 16, 128), F32),
             pltpu.VMEM((nr, shells, cycles * block), BF16),
             pltpu.VMEM((nr, shells, cycles * block), BF16),
-            pltpu.VMEM((nr, 2, shells, degrees), F32),
-            pltpu.VMEM((2, degrees, 2 * nr * shells), BF16),
+            pltpu.VMEM((nr, 2, shells, degrees), BF16),
+            pltpu.VMEM((2, degrees, nr * shells), BF16),
             pltpu.VMEM((nl, 2 * owned, block), F32),
             pltpu.VMEM((nl, 2 * owned, block), wire),
             pltpu.VMEM((nl, 2 * owned, block), wire),
@@ -288,16 +337,17 @@
             dma((nl,)), dma((nl,)), dma((nr,)), dma((nr,)),
         ],
         compiler_params=pltpu.CompilerParams(
-            collective_id=0, has_side_effects=True, vmem_limit_bytes=40 * 2**20
+            collective_id=0, has_side_effects=True, vmem_limit_bytes=60 * 2**20
         ),
-    )(pressure, residual, inv_visc, thermal, compress[None, :], legendre, kernels, table)
-    response = response.reshape(2, owned, 2, orders)
-    return (
-        jnp.transpose(pressure_new, (1, 0, 2)),
-        jnp.transpose(residual_new, (1, 0, 2)),
-        response[0],
-        response[1],
-    )
+    )(*operands)
+    return pl.pallas_call(
+        placed,
+        out_shape=outputs,
+        in_specs=[anywhere] * 4,
+        out_specs=(anywhere,) * 4,
+        scratch_shapes=[dma((4,))],
+        compiler_params=pltpu.CompilerParams(vmem_limit_bytes=60 * 2**20),
+    )(*results)
 
 
 def solution(mesh):

time: 40.6 us -> 51.7 us (1.27)
  Pallas kernels: 29.1 us -> 50.9 us
  local copies, waits for them, and re-layouts: 10.5 us -> 0 us
    pallas_call x1 -> x2, Pallas kernels: 29.1 us -> 50.9 us  [the longest x1 29.9 us: on_device(): pl.pallas_call(functools.partial(kernel, nr, nl), out_shape=outputs, in_s...]
    unnamed x18 -> x0, local copies, waits for them, and re-layouts: 9.11 us -> none
    squeeze x2 -> x0, local copies, waits for them, and re-layouts: 1.34 us -> none  [the longest x1 0.67 us: on_device(): response[1]]
where the time goes in v2:
time: 51.7 us; the launch traced here: 51.5 us
  Pallas kernels  50.9 us (98%)
  between operations  0.64 us (1%)
    pallas_call x1, Pallas kernels, on_device(): pl.pallas_call(functools.partial(kernel, nr, nl), out_shape=outputs, in_s...  29.9 us
    pallas_call x1, Pallas kernels, on_device(): pl.pallas_call(placed, out_shape=outputs, in_specs=[anywhere] * 4, out_sp...  21 us

profile of v2, /device:TPU:0, one launch (start us, length us, event | category | flops | bytes accessed | tf_op | source)
XLA Modules:
  0.0 51.5 jit_solution(3421366368990407962)
XLA Ops:
  0.6 29.9 %shard_map.111 = (f32[32,4,512]{2,1,0:T(4,128)}, f32[32,4,512]{2,1,0:T(4,128)}, f32[32,2,256]{2,1,0:T(2,128)}, f32[32,2,256]{2,1,0:T(2,128)}) custom-call(f32[32,4,512]{2,1,0:T(4,128)} %pres_hbm.1, f32[32,4,512]{2,1,0:T(4,128)} %res_hbm.1, f32[32,4,512]{2,1,0:T(4,128)} %visc_hbm.1, f32[32,4,512]{2,1,0:T(4,128)} %therm_hbm.1, f32[1,32]{1,0:T(1,128)} %bitcast.1, ...), custom_call_target="tpu_custom_call" | custom-call | tf_op jit(solution)/shard_map/pallas_call | solution.py:310
  30.5 21.0 %shard_map.112 = (f32[32,4,512]{2,1,0:T(4,128)}, f32[32,4,512]{2,1,0:T(4,128)}, f32[32,2,256]{2,1,0:T(2,128)}, f32[32,2,256]{2,1,0:T(2,128)}) custom-call(f32[32,4,512]{2,1,0:T(4,128)} %get-tuple-element.8.refs_0_, f32[32,4,512]{2,1,0:T(4,128)} %get-tuple-element.9.refs_1_, f32[32,2,256]{2,1,0:T(2,128)} %get-tuple-element.10.refs_2_, ...), custom_call_target="tpu_custom_call" | custom-call | tf_op jit(solution)/shard_map/pallas_call | solution.py:343

commit v3 on v2

--- a/solution.py
+++ b/solution.py
@@ -100,10 +100,6 @@
         (shell_send, shell_recv, shell_ss, shell_rs, "radial", ri, nr),
     )
     for sender, receiver, ss, rs, axis, me, n in sides:
-        @pl.when(me > 0)
-        def _():
-            edge(sender, receiver, ss, rs, 0, axis, lax.rem(me + n - 1, n)).start()
-
         @pl.when(me < n - 1)
         def _():
             edge(sender, receiver, ss, rs, 1, axis, lax.rem(me + 1, n)).start()
@@ -124,37 +120,35 @@
         term = folded(r[a] * r[a])
         squares = term if squares is None else squares + term
 
-    for sender, receiver, ss, rs, axis, me, n in sides:
-        @pl.when(me < n - 1)
-        def _():
-            edge(sender, receiver, ss, rs, 0, axis, lax.rem(me + 1, n)).wait_recv()
-
-        @pl.when(me == n - 1)
-        def _():
-            receiver[0] = jnp.zeros(receiver.shape[1:], F32)
-
-        @pl.when(me > 0)
-        def _():
-            edge(sender, receiver, ss, rs, 1, axis, lax.rem(me + n - 1, n)).wait_recv()
-
-        @pl.when(me == 0)
-        def _():
-            receiver[1] = jnp.zeros(receiver.shape[1:], F32)
-
-    image = []
+    inner = []
     curvature = None
     for a in range(cycles):
         x = r[a]
-        up = jnp.where(row == shells - 1, shell_recv[0, a : a + 1, :], pltpu.roll(x, shells - 1, 0))
-        down = jnp.where(row == 0, shell_recv[1, a : a + 1, :], pltpu.roll(x, 1, 0))
-        following = r[a + 1] if a + 1 < cycles else cycle_recv[0]
-        preceding = r[a - 1] if a > 0 else cycle_recv[1]
-        beside = up + down + following + preceding
+        beside = jnp.where(row == shells - 1, 0.0, pltpu.roll(x, shells - 1, 0))
+        beside = beside + jnp.where(row == 0, 0.0, pltpu.roll(x, 1, 0))
+        if a + 1 < cycles:
+            beside = beside + r[a + 1]
+        if a > 0:
+            beside = beside + r[a - 1]
         beside = beside + pltpu.roll(x, 1, 1) + pltpu.roll(x, nlon - 1, 1)
         y = (6.0 + visc[:, a, :]) * x - beside
-        image.append(y)
+        inner.append(y)
         term = folded(x * y)
         curvature = term if curvature is None else curvature + term
+
+    for sender, receiver, ss, rs, axis, me, n in sides:
+        @pl.when(me > 0)
+        def _():
+            edge(sender, receiver, ss, rs, 1, axis, lax.rem(me + n - 1, n)).wait_recv()
+
+        @pl.when(me == 0)
+        def _():
+            receiver[1] = jnp.zeros(receiver.shape[1:], F32)
+
+    across = folded(r[0] * cycle_recv[1])
+    for a in range(cycles):
+        across = across + folded(r[a][0:8] * jnp.where(row[0:8] == 0, shell_recv[1, a : a + 1, :], 0.0))
+    curvature = curvature - 2.0 * across
 
     dot_r[0, 0:8] = squares
     dot_r[0, 8:16] = curvature
@@ -181,6 +175,11 @@
         for d in range(1, nl)
     ]
     later += copies
+    for sender, receiver, ss, rs, axis, me, n in sides:
+        @pl.when(me > 0)
+        def _():
+            edge(sender, receiver, ss, rs, 0, axis, lax.rem(me + n - 1, n)).start()
+
     for copy in copies:
         copy.wait_recv()
     total = dot_l[0]
@@ -230,9 +229,24 @@
         target = lax.rem(li + d, nl)
         copies.append(send(wire.at[target], terms.at[d], term_ss.at[d], term_rs.at[d], "lateral", target))
     later += copies
-    for a in range(cycles):
+    for sender, receiver, ss, rs, axis, me, n in sides:
+        @pl.when(me < n - 1)
+        def _():
+            edge(sender, receiver, ss, rs, 0, axis, lax.rem(me + 1, n)).wait_recv()
+
+        @pl.when(me == n - 1)
+        def _():
+            receiver[0] = jnp.zeros(receiver.shape[1:], F32)
+
+    for a in range(cycles):
+        image = inner[a] - jnp.where(row == shells - 1, shell_recv[0, a : a + 1, :], 0.0)
+        image = image - jnp.where(row == 0, shell_recv[1, a : a + 1, :], 0.0)
+        if a == 0:
+            image = image - cycle_recv[1]
+        if a == cycles - 1:
+            image = image - cycle_recv[0]
         pres_out[:, a, :] = pressure_new[a]
-        res_out[:, a, :] = r[a] - alpha * image[a]
+        res_out[:, a, :] = r[a] - alpha * image
     stores = [
         pltpu.make_async_copy(pres_out, pres_hbm_out, store_sem.at[0]),
         pltpu.make_async_copy(res_out, res_hbm_out, store_sem.at[1]),
@@ -282,12 +296,16 @@
 
 
 def placed(*refs):
-    sources, targets, sem = refs[:4], refs[4:8], refs[8]
-    copies = [pltpu.make_async_copy(a, b, sem.at[i]) for i, (a, b) in enumerate(zip(sources, targets))]
-    for copy in copies:
-        copy.start()
-    for copy in copies:
-        copy.wait()
+    sources, targets, held, load_sem, store_sem = refs[:4], refs[4:8], refs[8:12], refs[12], refs[13]
+    loads = [pltpu.make_async_copy(a, b, load_sem.at[i]) for i, (a, b) in enumerate(zip(sources, held))]
+    stores = [pltpu.make_async_copy(a, b, store_sem.at[i]) for i, (a, b) in enumerate(zip(held, targets))]
+    for load in loads:
+        load.start()
+    for load, store in zip(loads, stores):
+        load.wait()
+        store.start()
+    for store in stores:
+        store.wait()
 
 
 def on_device(pressure, residual, inv_visc, thermal, compress, legendre, kernels):
@@ -345,7 +363,7 @@
         out_shape=outputs,
         in_specs=[anywhere] * 4,
         out_specs=(anywhere,) * 4,
-        scratch_shapes=[dma((4,))],
+        scratch_shapes=[*(pltpu.VMEM(x.shape, x.dtype) for x in outputs), dma((4,)), dma((4,))],
         compiler_params=pltpu.CompilerParams(vmem_limit_bytes=60 * 2**20),
     )(*results)
 

time: 51.7 us -> 31.3 us (0.61)
  Pallas kernels: 50.9 us -> 30.5 us
    pallas_call x1, Pallas kernels: 21 us -> 1.84 us  [on_device(): pl.pallas_call(placed, out_shape=outputs, in_specs=[anywhere] * 4, out_sp...]
    pallas_call x1, Pallas kernels: 29.9 us -> 28.7 us  [on_device(): pl.pallas_call(functools.partial(kernel, nr, nl), out_shape=outputs, in_s...]
where the time goes in v3:
time: 31.3 us; the launch traced here: 31.2 us
  Pallas kernels  30.5 us (97%)
  between operations  0.64 us (2%)
    pallas_call x1, Pallas kernels, on_device(): pl.pallas_call(functools.partial(kernel, nr, nl), out_shape=outputs, in_s...  28.7 us
    pallas_call x1, Pallas kernels, on_device(): pl.pallas_call(placed, out_shape=outputs, in_specs=[anywhere] * 4, out_sp...  1.84 us

profile of v3, /device:TPU:0, one launch (start us, length us, event | category | flops | bytes accessed | tf_op | source)
XLA Modules:
  0.0 31.2 jit_solution(2960106673849814351)
XLA Ops:
  0.6 28.7 %shard_map.111 = (f32[32,4,512]{2,1,0:T(4,128)}, f32[32,4,512]{2,1,0:T(4,128)}, f32[32,2,256]{2,1,0:T(2,128)}, f32[32,2,256]{2,1,0:T(2,128)}) custom-call(f32[32,4,512]{2,1,0:T(4,128)} %pres_hbm.1, f32[32,4,512]{2,1,0:T(4,128)} %res_hbm.1, f32[32,4,512]{2,1,0:T(4,128)} %visc_hbm.1, f32[32,4,512]{2,1,0:T(4,128)} %therm_hbm.1, f32[1,32]{1,0:T(1,128)} %bitcast.1, ...), custom_call_target="tpu_custom_call" | custom-call | tf_op jit(solution)/shard_map/pallas_call | solution.py:328
  29.3 1.8 %shard_map.112 = (f32[32,4,512]{2,1,0:T(4,128)}, f32[32,4,512]{2,1,0:T(4,128)}, f32[32,2,256]{2,1,0:T(2,128)}, f32[32,2,256]{2,1,0:T(2,128)}) custom-call(f32[32,4,512]{2,1,0:T(4,128)} %get-tuple-element.8.refs_0_, f32[32,4,512]{2,1,0:T(4,128)} %get-tuple-element.9.refs_1_, f32[32,2,256]{2,1,0:T(2,128)} %get-tuple-element.10.refs_2_, ...), custom_call_target="tpu_custom_call" | custom-call | tf_op jit(solution)/shard_map/pallas_call | solution.py:361

commit v4 on v3

--- a/solution.py
+++ b/solution.py
@@ -150,8 +150,8 @@
         across = across + folded(r[a][0:8] * jnp.where(row[0:8] == 0, shell_recv[1, a : a + 1, :], 0.0))
     curvature = curvature - 2.0 * across
 
-    dot_r[0, 0:8] = squares
-    dot_r[0, 8:16] = curvature
+    dot_r[0, 0:1] = jnp.sum(squares, axis=0, keepdims=True)
+    dot_r[0, 1:2] = jnp.sum(curvature, axis=0, keepdims=True)
     copies = [
         send(dot_r.at[0], dot_r.at[d], dotr_ss.at[d], dotr_rs.at[d], "radial", lax.rem(ri + d, nr))
         for d in range(1, nr)
@@ -185,7 +185,7 @@
     total = dot_l[0]
     for d in range(1, nl):
         total = total + dot_l[d]
-    alpha = jnp.sum(total[0:8], keepdims=True) / jnp.sum(total[8:16], keepdims=True)
+    alpha = jnp.sum(total[0:1], keepdims=True) / jnp.sum(total[1:2], keepdims=True)
 
     anomaly, pressure_new = [], []
     for a in range(cycles):
@@ -224,8 +224,9 @@
             piece = value[b * owned : (b + 1) * owned]
             part[b, k * owned : (k + 1) * owned, :] = piece
             wire[b, k * owned : (k + 1) * owned, :] = piece.astype(wire.dtype)
+    far_first = sorted(range(1, nl), key=lambda d: -min(d, nl - d))
     copies = []
-    for d in range(1, nl):
+    for d in far_first:
         target = lax.rem(li + d, nl)
         copies.append(send(wire.at[target], terms.at[d], term_ss.at[d], term_rs.at[d], "lateral", target))
     later += copies
@@ -254,12 +255,12 @@
     for store in stores:
         store.start()
     total = part[li]
-    for d in range(1, nl):
-        copies[d - 1].wait_recv()
+    for d, copy in zip(far_first, copies):
+        copy.wait_recv()
         total = total + terms[d].astype(F32)
     mine = pl.ds(pl.multiple_of(ri * block, block), block)
     for k in range(2):
-        final[k, :, mine] = total[k * owned : (k + 1) * owned]
+        final[k, :, mine] = total[k * owned : (k + 1) * owned].astype(final.dtype)
     copies = [
         send(final.at[:, :, mine], final.at[:, :, mine], fin_ss.at[d], fin_rs.at[d], "radial", lax.rem(ri + d, nr))
         for d in range(1, nr)
@@ -273,8 +274,8 @@
             device_id={"radial": origin}, device_id_type=MESH,
         ).wait_recv()
     for c in range(2):
-        geoid_out[:, c, :] = final[0, :, c * orders : (c + 1) * orders]
-        topo_out[:, c, :] = final[1, :, c * orders : (c + 1) * orders]
+        geoid_out[:, c, :] = final[0, :, c * orders : (c + 1) * orders].astype(F32)
+        topo_out[:, c, :] = final[1, :, c * orders : (c + 1) * orders].astype(F32)
     responses = [
         pltpu.make_async_copy(geoid_out, geoid_hbm_out, store_sem.at[2]),
         pltpu.make_async_copy(topo_out, topo_hbm_out, store_sem.at[3]),
@@ -333,15 +334,15 @@
         scratch_shapes=[
             *(pltpu.VMEM(x.shape, x.dtype) for x in operands),
             dma((8,)),
-            pltpu.VMEM((2, owned, 2 * orders), F32),
+            pltpu.VMEM((2, owned, 2 * orders), wire),
             *(pltpu.VMEM(x.shape, x.dtype) for x in outputs),
             dma((4,)),
             pltpu.VMEM((2, cycles, nlon), F32),
             pltpu.VMEM((2, cycles, nlon), F32),
             pltpu.VMEM((2, shells, nlon), F32),
             pltpu.VMEM((2, shells, nlon), F32),
-            pltpu.VMEM((nr, 16, 128), F32),
-            pltpu.VMEM((nl, 16, 128), F32),
+            pltpu.VMEM((nr, 2, 128), F32),
+            pltpu.VMEM((nl, 2, 128), F32),
             pltpu.VMEM((nr, shells, cycles * block), BF16),
             pltpu.VMEM((nr, shells, cycles * block), BF16),
             pltpu.VMEM((nr, 2, shells, degrees), BF16),

time: 31.3 us -> 31.8 us (1.016)
  Pallas kernels: 30.5 us -> 31 us
    pallas_call x1, Pallas kernels: 28.7 us -> 29.2 us  [on_device(): pl.pallas_call(functools.partial(kernel, nr, nl), out_shape=outputs, in_s...]
where the time goes in v4:
time: 31.8 us; the launch traced here: 31.6 us
  Pallas kernels  31 us (97%)
  between operations  0.64 us (2%)
    pallas_call x1, Pallas kernels, on_device(): pl.pallas_call(functools.partial(kernel, nr, nl), out_shape=outputs, in_s...  29.2 us
    pallas_call x1, Pallas kernels, on_device(): pl.pallas_call(placed, out_shape=outputs, in_specs=[anywhere] * 4, out_sp...  1.84 us

profile of v4, /device:TPU:0, one launch (start us, length us, event | category | flops | bytes accessed | tf_op | source)
XLA Modules:
  0.0 31.6 jit_solution(14856513082152226659)
XLA Ops:
  0.6 29.2 %shard_map.111 = (f32[32,4,512]{2,1,0:T(4,128)}, f32[32,4,512]{2,1,0:T(4,128)}, f32[32,2,256]{2,1,0:T(2,128)}, f32[32,2,256]{2,1,0:T(2,128)}) custom-call(f32[32,4,512]{2,1,0:T(4,128)} %pres_hbm.1, f32[32,4,512]{2,1,0:T(4,128)} %res_hbm.1, f32[32,4,512]{2,1,0:T(4,128)} %visc_hbm.1, f32[32,4,512]{2,1,0:T(4,128)} %therm_hbm.1, f32[1,32]{1,0:T(1,128)} %bitcast.1, ...), custom_call_target="tpu_custom_call" | custom-call | tf_op jit(solution)/shard_map/pallas_call | solution.py:329
  29.8 1.8 %shard_map.112 = (f32[32,4,512]{2,1,0:T(4,128)}, f32[32,4,512]{2,1,0:T(4,128)}, f32[32,2,256]{2,1,0:T(2,128)}, f32[32,2,256]{2,1,0:T(2,128)}) custom-call(f32[32,4,512]{2,1,0:T(4,128)} %get-tuple-element.8.refs_0_, f32[32,4,512]{2,1,0:T(4,128)} %get-tuple-element.9.refs_1_, f32[32,2,256]{2,1,0:T(2,128)} %get-tuple-element.10.refs_2_, ...), custom_call_target="tpu_custom_call" | custom-call | tf_op jit(solution)/shard_map/pallas_call | solution.py:362

commit v5 on v3

--- a/solution.py
+++ b/solution.py
@@ -214,6 +214,7 @@
 
     stack = jnp.concatenate([spec_recv[d] for d in range(nr)], axis=0)
     first = pl.multiple_of(lax.rem(ri * block, orders), block)
+    sums = [[], []]
     for k in range(2):
         weighted = jnp.dot(ker_t[k], stack, preferred_element_type=F32)
         value = None
@@ -222,13 +223,12 @@
             value = term if value is None else value + term
         for b in range(nl):
             piece = value[b * owned : (b + 1) * owned]
-            part[b, k * owned : (k + 1) * owned, :] = piece
-            wire[b, k * owned : (k + 1) * owned, :] = piece.astype(wire.dtype)
-    copies = []
-    for d in range(1, nl):
-        target = lax.rem(li + d, nl)
-        copies.append(send(wire.at[target], terms.at[d], term_ss.at[d], term_rs.at[d], "lateral", target))
-    later += copies
+            part[k, b] = piece
+            wire[k, b] = piece.astype(wire.dtype)
+        for d in range(1, nl):
+            target, slot = lax.rem(li + d, nl), k * nl + d
+            sums[k].append(send(wire.at[k, target], terms.at[k, d], term_ss.at[slot], term_rs.at[slot], "lateral", target))
+        later += sums[k]
     for sender, receiver, ss, rs, axis, me, n in sides:
         @pl.when(me < n - 1)
         def _():
@@ -253,25 +253,26 @@
     ]
     for store in stores:
         store.start()
-    total = part[li]
-    for d in range(1, nl):
-        copies[d - 1].wait_recv()
-        total = total + terms[d].astype(F32)
     mine = pl.ds(pl.multiple_of(ri * block, block), block)
+    copies = []
     for k in range(2):
-        final[k, :, mine] = total[k * owned : (k + 1) * owned]
-    copies = [
-        send(final.at[:, :, mine], final.at[:, :, mine], fin_ss.at[d], fin_rs.at[d], "radial", lax.rem(ri + d, nr))
-        for d in range(1, nr)
-    ]
-    for d in range(1, nr):
-        origin = lax.rem(ri + nr - d, nr)
-        theirs = pl.ds(pl.multiple_of(origin * block, block), block)
-        pltpu.make_async_remote_copy(
-            src_ref=final.at[:, :, theirs], dst_ref=final.at[:, :, theirs],
-            send_sem=fin_ss.at[d], recv_sem=fin_rs.at[d],
-            device_id={"radial": origin}, device_id_type=MESH,
-        ).wait_recv()
+        total = part[k, li]
+        for d in range(1, nl):
+            sums[k][d - 1].wait_recv()
+            total = total + terms[k, d].astype(F32)
+        final[k, :, mine] = total
+        for d in range(1, nr):
+            here, slot = final.at[k, :, mine], k * nr + d
+            copies.append(send(here, here, fin_ss.at[slot], fin_rs.at[slot], "radial", lax.rem(ri + d, nr)))
+    for k in range(2):
+        for d in range(1, nr):
+            origin, slot = lax.rem(ri + nr - d, nr), k * nr + d
+            theirs = pl.ds(pl.multiple_of(origin * block, block), block)
+            pltpu.make_async_remote_copy(
+                src_ref=final.at[k, :, theirs], dst_ref=final.at[k, :, theirs],
+                send_sem=fin_ss.at[slot], recv_sem=fin_rs.at[slot],
+                device_id={"radial": origin}, device_id_type=MESH,
+            ).wait_recv()
     for c in range(2):
         geoid_out[:, c, :] = final[0, :, c * orders : (c + 1) * orders]
         topo_out[:, c, :] = final[1, :, c * orders : (c + 1) * orders]
@@ -346,13 +347,13 @@
             pltpu.VMEM((nr, shells, cycles * block), BF16),
             pltpu.VMEM((nr, 2, shells, degrees), BF16),
             pltpu.VMEM((2, degrees, nr * shells), BF16),
-            pltpu.VMEM((nl, 2 * owned, block), F32),
-            pltpu.VMEM((nl, 2 * owned, block), wire),
-            pltpu.VMEM((nl, 2 * owned, block), wire),
+            pltpu.VMEM((2, nl, owned, block), F32),
+            pltpu.VMEM((2, nl, owned, block), wire),
+            pltpu.VMEM((2, nl, owned, block), wire),
             dma((2,)), dma((2,)), dma((2,)), dma((2,)),
             dma((nr,)), dma((nr,)), dma((nl,)), dma((nl,)),
             dma((nr,)), dma((nr,)), dma((nr,)), dma((nr,)),
-            dma((nl,)), dma((nl,)), dma((nr,)), dma((nr,)),
+            dma((2 * nl,)), dma((2 * nl,)), dma((2 * nr,)), dma((2 * nr,)),
         ],
         compiler_params=pltpu.CompilerParams(
             collective_id=0, has_side_effects=True, vmem_limit_bytes=60 * 2**20

time: 31.3 us -> 32.1 us (1.026)
  Pallas kernels: 30.5 us -> 31.3 us
    pallas_call x1, Pallas kernels: 28.7 us -> 29.4 us  [on_device(): pl.pallas_call(functools.partial(kernel, nr, nl), out_shape=outputs, in_s...]
where the time goes in v5:
time: 32.1 us; the launch traced here: 31.9 us
  Pallas kernels  31.3 us (98%)
  between operations  0.64 us (2%)
    pallas_call x1, Pallas kernels, on_device(): pl.pallas_call(functools.partial(kernel, nr, nl), out_shape=outputs, in_s...  29.4 us
    pallas_call x1, Pallas kernels, on_device(): pl.pallas_call(placed, out_shape=outputs, in_specs=[anywhere] * 4, out_sp...  1.84 us

profile of v5, /device:TPU:0, one launch (start us, length us, event | category | flops | bytes accessed | tf_op | source)
XLA Modules:
  0.0 31.9 jit_solution(5227685539652294392)
XLA Ops:
  0.6 29.4 %shard_map.111 = (f32[32,4,512]{2,1,0:T(4,128)}, f32[32,4,512]{2,1,0:T(4,128)}, f32[32,2,256]{2,1,0:T(2,128)}, f32[32,2,256]{2,1,0:T(2,128)}) custom-call(f32[32,4,512]{2,1,0:T(4,128)} %pres_hbm.1, f32[32,4,512]{2,1,0:T(4,128)} %res_hbm.1, f32[32,4,512]{2,1,0:T(4,128)} %visc_hbm.1, f32[32,4,512]{2,1,0:T(4,128)} %therm_hbm.1, f32[1,32]{1,0:T(1,128)} %bitcast.1, ...), custom_call_target="tpu_custom_call" | custom-call | tf_op jit(solution)/shard_map/pallas_call | solution.py:329
  30.1 1.8 %shard_map.112 = (f32[32,4,512]{2,1,0:T(4,128)}, f32[32,4,512]{2,1,0:T(4,128)}, f32[32,2,256]{2,1,0:T(2,128)}, f32[32,2,256]{2,1,0:T(2,128)}) custom-call(f32[32,4,512]{2,1,0:T(4,128)} %get-tuple-element.8.refs_0_, f32[32,4,512]{2,1,0:T(4,128)} %get-tuple-element.9.refs_1_, f32[32,2,256]{2,1,0:T(2,128)} %get-tuple-element.10.refs_2_, ...), custom_call_target="tpu_custom_call" | custom-call | tf_op jit(solution)/shard_map/pallas_call | solution.py:362
